TPU v7x, 32 devices: a whole 2x2x4 slice. The times are simulated.
32 devices in a mesh: slab: 4 (over y, core), tile: 8 (over z, x).
Axes of the slice: x: 2, y: 2, z: 4, core: 2. Of those that a mesh axis runs over, the one named last changes fastest.
Arguments:
- volume: float32 [768, 256, 128], P('tile', 'slab'), may hold values from 0 to 2
- footprints: bfloat16 [32, 128, 128], replicated, may hold values from -0.02734375 to 0.02734375
- foot_index: int32 [768, 8], P('tile'), may hold values from 0 to 31
- ray_block: int32 [768, 8], replicated, may hold values from 0 to 15, as said below
- ray_slot: int32 [16], replicated, may hold values from 0 to 15, as said below
- measured: float32 [16, 256, 128], P('tile', 'slab'), may hold values from -6 to 6
- weights: float32 [16, 256, 128], P('tile', 'slab'), may hold values from 0.25 to 4
Outputs:
- updated_volume: float32 [768, 256, 128], P('tile', 'slab')
Inputs may be any that keep to these rules, and one draw needn't show every extreme that they name: A permutation of the 16 ray blocks; ray block b is held by index ray_slot[b] // 2 of tile, and its rows of measured and weights are row ray_slot[b]. `ray_block`: the crossings of the rows held by one index of tile name at most 4 distinct ray blocks, no two of them held by the same owner.
All inputs are finite; a program needn't handle non-finite values.
Results may differ from a plain program's by a relative error of at most 0.002.
Values may be sent and summed in bfloat16 or wider, within the bound.
A program may use at most 128 MiB of HBM per device.

v0:
```python
import math

import jax
import jax.numpy as jnp
from jax import lax
from jax.sharding import PartitionSpec as P

smoothing = 0.04
step_length = 2.0
variation_weight = 1.0
block_limit = 32


def from_behind(block, axis, distance):
    devices = range(lax.axis_size(axis))
    route = [(i - distance, i) for i in devices if i - distance in devices]
    return lax.ppermute(block, axis, route)


def flux_parts(grad_rows, grad_slices, grad_cols):
    magnitude = jnp.sqrt(
        grad_rows * grad_rows + grad_slices * grad_slices + grad_cols * grad_cols + smoothing
    )
    return (grad_rows / magnitude, grad_slices / magnitude, grad_cols / magnitude)


def column_grad(density):
    return jnp.concatenate(
        [density[:, :, 1:] - density[:, :, :-1], jnp.zeros_like(density[:, :, :1])], axis=2
    )


def column_div(flux):
    return jnp.concatenate([jnp.zeros_like(flux[:, :, :1]), flux[:, :, :-1]], axis=2) - flux


def per_device(volume, footprints, foot_index, ray_block, ray_slot, measured, weights):
    row_count, slice_count, column_count = volume.shape
    ray_width = footprints.shape[2]
    crossings = foot_index.shape[1]
    owners = lax.axis_size("tile")
    owned_count = measured.shape[0]
    position = lax.axis_index("tile")
    layer = lax.axis_index("slab")
    my_blocks = lax.dynamic_slice_in_dim(ray_block, position * row_count, row_count, 0)
    my_slots = jnp.take(ray_slot, my_blocks, axis=0)
    targets = my_slots // owned_count
    touch_count = owners // 2
    labels = jnp.arange(owners, dtype=jnp.int32)
    present = jnp.any(targets.reshape(-1)[:, None] == labels[None, :], axis=0)
    rank = jnp.cumsum(present.astype(jnp.int32)) - 1
    compact_targets = jnp.take(rank, targets, axis=0)
    compact_labels = jnp.arange(touch_count, dtype=jnp.int32)
    rounded = volume.astype(jnp.bfloat16)
    block_rows = math.gcd(row_count, block_limit)
    turns = row_count // block_rows
    pixel_groups = rounded.reshape(turns, block_rows, slice_count, column_count)
    offset_groups = foot_index.reshape(turns, block_rows, crossings)
    target_groups = targets.reshape(turns, block_rows, crossings)
    compact_groups = compact_targets.reshape(turns, block_rows, crossings)

    def project(running_sum, inputs):
        pixels, offsets, destinations = inputs
        stencil = jnp.take(footprints, offsets, axis=0)
        partial_value = jnp.einsum(
            "rzp,rkpq->rkzq", pixels, stencil, preferred_element_type=jnp.float32
        )
        flat = partial_value.reshape(block_rows * crossings, slice_count * ray_width)
        high = flat.astype(jnp.bfloat16)
        low = (flat - high.astype(jnp.float32)).astype(jnp.bfloat16)
        selector = (destinations.reshape(-1)[:, None] == compact_labels[None, :]).astype(
            jnp.bfloat16
        )
        dims = (((0,), (0,)), ((), ()))
        contrib = lax.dot_general(selector, high, dims, preferred_element_type=jnp.float32)
        contrib = contrib + lax.dot_general(selector, low, dims, preferred_element_type=jnp.float32)
        return (running_sum + contrib, None)

    start = jnp.zeros((touch_count, slice_count * ray_width), jnp.float32)
    compact_totals, _ = lax.scan(project, start, (pixel_groups, offset_groups, compact_groups))
    picked = jnp.take(compact_totals, jnp.clip(rank, 0, touch_count - 1), axis=0)
    totals = jnp.where(present[:, None], picked, 0.0)
    totals = totals.reshape(owners, slice_count, ray_width)
    arrived = lax.all_to_all(totals, "tile", split_axis=0, concat_axis=0, tiled=True)
    every_slot = jnp.take(ray_slot, ray_block, axis=0).reshape(owners, row_count * crossings)
    owned_here = every_slot // owned_count == position
    local_index = jnp.max(jnp.where(owned_here, every_slot % owned_count, 0), axis=1)
    chooser = jnp.arange(owned_count, dtype=jnp.int32)[:, None] == local_index[None, :]
    own_sums = jnp.sum(jnp.where(chooser[:, :, None, None], arrived[None], 0.0), axis=1)
    residual = (weights * (own_sums - measured)).astype(jnp.bfloat16)
    returned = lax.all_to_all(
        jnp.take(residual, local_index, axis=0), "tile", split_axis=0, concat_axis=0, tiled=True
    )

    def backproject(running, inputs):
        offsets, destinations = inputs
        stencil = jnp.take(footprints, offsets, axis=0)
        values = jnp.take(returned, destinations, axis=0)
        return (
            running,
            jnp.einsum("rkzq,rkpq->rzp", values, stencil, preferred_element_type=jnp.float32),
        )

    _, pieces = lax.scan(backproject, jnp.zeros((), jnp.float32), (offset_groups, target_groups))
    data_grad = pieces.reshape(row_count, slice_count, column_count)
    total_rows = row_count * owners
    total_slices = slice_count * lax.axis_size("slab")
    row_ids = position * row_count + jnp.arange(row_count, dtype=jnp.int32)
    slice_ids = layer * slice_count + jnp.arange(slice_count, dtype=jnp.int32)
    next_row = from_behind(volume[:1], "tile", -1)
    next_slice = from_behind(volume[:, :1], "slab", -1)
    grad_rows = jnp.concatenate([volume[1:], next_row], axis=0) - volume
    grad_rows = jnp.where((row_ids == total_rows - 1)[:, None, None], 0.0, grad_rows)
    grad_slices = jnp.concatenate([volume[:, 1:], next_slice], axis=1) - volume
    grad_slices = jnp.where((slice_ids == total_slices - 1)[None, :, None], 0.0, grad_slices)
    grad_cols = column_grad(volume)
    flux_rows, flux_slices, flux_cols = flux_parts(grad_rows, grad_slices, grad_cols)
    prev_row = from_behind(flux_rows[-1:], "tile", 1)
    prev_slice = from_behind(flux_slices[:, -1:], "slab", 1)
    variation = jnp.concatenate([prev_row, flux_rows[:-1]], axis=0) - flux_rows
    variation = variation + (
        jnp.concatenate([prev_slice, flux_slices[:, :-1]], axis=1) - flux_slices
    )
    variation = variation + column_div(flux_cols)
    updated = volume - step_length * (data_grad + variation_weight * variation)
    return jnp.maximum(updated, 0.0)


def solution(mesh):
    in_specs = (
        P("tile", "slab", None),
        P(),
        P("tile", None),
        P(),
        P(),
        P("tile", "slab", None),
        P("tile", "slab", None),
    )
    out_specs = P("tile", "slab", None)
    return jax.shard_map(
        per_device, mesh=mesh, in_specs=in_specs, out_specs=out_specs, check_vma=False
    )
```

profile of v0, /device:TPU:0, one launch (start us, length us, event | category | flops | bytes accessed | tf_op | source)
XLA Modules:
  0.0 268.2 jit_solution(14579264922321679932)
XLA Ops:
  0.0 1.0 slice.36
  1.0 1.3 collective-permute-start.1
  2.3 0.8 slice.34
  3.1 1.3 collective-permute-start
  4.4 5.6 %slice_subtract_fusion = f32[96,64,127]{2,1,0:T(8,128)} fusion(f32[96,64,128]{2,1,0:T(8,128)} %param.13), kind=kLoop, calls=%fused_computation.58 | loop fusion | flops 780288 | bytes 9363456 | tf_op jit(solution)/shard_map/sub | solution.py:29
  10.0 0.7 fusion.63
  10.7 10.0 %select_select_fusion.2 = s32[96,8]{0,1:T(8,128)S(1)} fusion(s32[768,8]{0,1:T(8,128)S(1)} %copy-done.5, s32[]{:T(128)S(6)} %select_n.175, s32[]{:T(128)} %bitcast.8, s32[]{:T(128)} %bitcast.9, s32[]{:T(128)} %bitcast.10, s32[]{:T(128)} %bitcast.11, s32[]{:T(128)} %bitcast.12, s32[]{:T(128)} %bitcast.13, s32[]{:T(128)} %bitcast.14, s32[]{:T(128)} %bitcast.15, ...), kind=kLoop, calls=%fused_computation.102 | loop fusion | flops 28416 | bytes 6212 | tf_op jit(solution)/shard_map/jit(_take)/select_n | solution.py:46
  20.7 0.1 copy.21
  20.8 0.1 select_n.186
  20.9 0.1 fusion.52
  21.1 0.2 reduce-window.4
  21.3 10.0 %fusion.50 = s32[768]{0:T(1024)S(1)} fusion(s32[768,8]{0,1:T(8,128)S(1)} %copy-done.5, s32[]{:T(128)} %bitcast.8, s32[]{:T(128)} %bitcast.9, s32[]{:T(128)} %bitcast.10, s32[]{:T(128)} %bitcast.11, s32[]{:T(128)} %bitcast.12, s32[]{:T(128)} %bitcast.13, s32[]{:T(128)} %bitcast.14, s32[]{:T(128)} %bitcast.15, s32[]{:T(128)} %bitcast.16, s32[]{:T(128)} %bitcast.17, ...), kind=kLoop, calls=%fused_computation.80 | loop fusion | flops 361728 | bytes 27716 | tf_op jit(solution)/shard_map/reduce_max | solution.py:87
  31.3 0.7 fusion.62
  32.0 0.1 reduce_max.20
  32.2 15.1 %select_select_fusion.1 = s32[96,8]{0,1:T(8,128)S(1)} fusion(s32[]{:T(128)} %bitcast.27, s32[]{:T(128)} %bitcast.28, s32[]{:T(128)} %bitcast.29, s32[]{:T(128)} %bitcast.30, s32[]{:T(128)} %bitcast.31, s32[]{:T(128)} %bitcast.32, s32[]{:T(128)} %bitcast.33, s32[]{:T(128)} %bitcast.34, s32[]{:T(128)} %bitcast.23, s32[]{:T(128)} %bitcast.22, s32[]{:T(128)} %bitcast.21, ...), kind=kLoop, calls=%fused_computation.101 | loop fusion | flops 56064 | bytes 6244 | tf_op jit(solution)/shard_map/jit(_take)/select_n | solution.py:52
  47.3 2.2 slice.35
  49.5 1.8 slice.33
  51.3 0.1 copy.28
  51.4 0.1 copy.23
  51.6 10.8 %pad_divide_fusion = (f32[96,64,128]{2,1,0:T(8,128)}, f32[96,64,128]{2,1,0:T(8,128)}, f32[96,64,128]{2,1,0:T(8,128)}, bf16[96,64,128]{2,1,0:T(8,128)(2,1)S(1)}) fusion(f32[96,64,127]{2,1,0:T(8,128)} %slice_subtract_fusion, f32[96,64,128]{2,1,0:T(8,128)} %param.13, f32[96,1,128]{2,1,0:T(1,128)S(1)} %collective-permute-done.1, f32[96,63,128]{2,1,0:T(8,128)} %slice.35, ...), kind=kLoop, calls=%fused_computation.59 | loop fusion | flops 12582912 | bytes 23568544 | tf_op jit(solution)/shard_map/div | solution.py:24
  62.4 99.2 %while.22 = (s32[]{:T(128)}, f32[4,8192]{1,0:T(4,128)S(1)}, s32[3,32,8]{2,1,0:T(8,128)S(1)}, s32[3,32,8]{2,1,0:T(8,128)S(1)}, bf16[32,128,128]{2,1,0:T(8,128)(2,...) while((s32[]{:T(128)}, f32[4,8192]{1,0:T(4,128)S(1)}, ...), condition=%wide.region_5.7_spmd.clone, body=%wide.region_4.6_spmd.clone.sunk | while | flops 583111168 | bytes 51401064 | solution.py:80
  62.4 0.1 reshape.426
  62.5 8.7 %gather_fusion.2 = bf16[256,128,128]{2,1,0:T(8,128)(2,1)} fusion(bf16[32,128,128]{2,1,0:T(8,128)(2,1)S(1)} %get-tuple-element.281, s32[1024]{0:T(1024)S(1)} %pad_clamp_fusion.10), kind=kCustom, calls=%fused_computation.clone.clone.1 | custom fusion | bytes 16778240 | tf_op jit(solution)/shard_map/while/body/eval_jaxpr/jit(_take)/gather | solution.py:64
  71.2 8.3 %fusion.79 = f32[32,8,64,128]{3,2,1,0:T(8,128)} fusion(bf16[32,8,128,128]{3,2,1,0:T(8,128)(2,1)} %bitcast.103, pred[32,8]{1,0:T(8,128)(4,1)S(1)} %get-tuple-element.260, bf16[3,32,64,128]{3,2,1,0:T(8,128)(2,1)S(1)} %get-tuple-element.282, s32[]{:T(128)} %get-tuple-element.269), kind=kOutput, calls=%fused_computation.33.clone.1 | convolution fusion | flops 541065216 | bytes 17305604 | tf_op jit(solution)/shard_map/while/body/eval_jaxpr/rzp,rkpq->rkzq/dot_general | solution.py:65
  79.5 0.1 eq.129
  79.6 7.9 %fusion.80 = f32[4,8192]{1,0:T(4,128)S(1)} fusion(f32[32,8,64,128]{3,2,1,0:T(8,128)} %fusion.79, s32[256]{0:T(256)S(1)} %eq.129), kind=kOutput, calls=%fused_computation.31.clone.1 | convolution fusion | flops 16778240 | bytes 8520704 | tf_op jit(solution)/shard_map/while/body/eval_jaxpr/dot_general | solution.py:75
  87.5 7.9 %fusion.81 = f32[4,8192]{1,0:T(4,128)S(1)} fusion(f32[4,8192]{1,0:T(4,128)S(1)} %fusion.80, f32[32,8,64,128]{3,2,1,0:T(8,128)} %fusion.79, f32[4,8192]{1,0:T(4,128)S(1)} %get-tuple-element.270, s32[256]{0:T(256)S(1)} %eq.129, pred[]{:T(512)S(6)} %compare.165), kind=kOutput, calls=%fused_computation.24.clone.1 | convolution fusion | flops 25265152 | bytes 8782849 | tf_op jit(solution)/shard_map/while/body/eval_jaxpr/dot_general | solution.py:76
  95.5 8.7 %gather_fusion.2 = bf16[256,128,128]{2,1,0:T(8,128)(2,1)} fusion(bf16[32,128,128]{2,1,0:T(8,128)(2,1)S(1)} %get-tuple-element.281, s32[1024]{0:T(1024)S(1)} %pad_clamp_fusion.10), kind=kCustom, calls=%fused_computation.clone.clone.1 | custom fusion | bytes 16778240 | tf_op jit(solution)/shard_map/while/body/eval_jaxpr/jit(_take)/gather | solution.py:64
  104.2 8.3 %fusion.79 = f32[32,8,64,128]{3,2,1,0:T(8,128)} fusion(bf16[32,8,128,128]{3,2,1,0:T(8,128)(2,1)} %bitcast.103, pred[32,8]{1,0:T(8,128)(4,1)S(1)} %get-tuple-element.260, bf16[3,32,64,128]{3,2,1,0:T(8,128)(2,1)S(1)} %get-tuple-element.282, s32[]{:T(128)} %get-tuple-element.269), kind=kOutput, calls=%fused_computation.33.clone.1 | convolution fusion | flops 541065216 | bytes 17305604 | tf_op jit(solution)/shard_map/while/body/eval_jaxpr/rzp,rkpq->rkzq/dot_general | solution.py:65
  112.6 0.1 eq.129
  112.7 7.9 %fusion.80 = f32[4,8192]{1,0:T(4,128)S(1)} fusion(f32[32,8,64,128]{3,2,1,0:T(8,128)} %fusion.79, s32[256]{0:T(256)S(1)} %eq.129), kind=kOutput, calls=%fused_computation.31.clone.1 | convolution fusion | flops 16778240 | bytes 8520704 | tf_op jit(solution)/shard_map/while/body/eval_jaxpr/dot_general | solution.py:75
  120.5 7.9 %fusion.81 = f32[4,8192]{1,0:T(4,128)S(1)} fusion(f32[4,8192]{1,0:T(4,128)S(1)} %fusion.80, f32[32,8,64,128]{3,2,1,0:T(8,128)} %fusion.79, f32[4,8192]{1,0:T(4,128)S(1)} %get-tuple-element.270, s32[256]{0:T(256)S(1)} %eq.129, pred[]{:T(512)S(6)} %compare.165), kind=kOutput, calls=%fused_computation.24.clone.1 | convolution fusion | flops 25265152 | bytes 8782849 | tf_op jit(solution)/shard_map/while/body/eval_jaxpr/dot_general | solution.py:76
  128.6 8.7 %gather_fusion.2 = bf16[256,128,128]{2,1,0:T(8,128)(2,1)} fusion(bf16[32,128,128]{2,1,0:T(8,128)(2,1)S(1)} %get-tuple-element.281, s32[1024]{0:T(1024)S(1)} %pad_clamp_fusion.10), kind=kCustom, calls=%fused_computation.clone.clone.1 | custom fusion | bytes 16778240 | tf_op jit(solution)/shard_map/while/body/eval_jaxpr/jit(_take)/gather | solution.py:64
  137.3 8.3 %fusion.79 = f32[32,8,64,128]{3,2,1,0:T(8,128)} fusion(bf16[32,8,128,128]{3,2,1,0:T(8,128)(2,1)} %bitcast.103, pred[32,8]{1,0:T(8,128)(4,1)S(1)} %get-tuple-element.260, bf16[3,32,64,128]{3,2,1,0:T(8,128)(2,1)S(1)} %get-tuple-element.282, s32[]{:T(128)} %get-tuple-element.269), kind=kOutput, calls=%fused_computation.33.clone.1 | convolution fusion | flops 541065216 | bytes 17305604 | tf_op jit(solution)/shard_map/while/body/eval_jaxpr/rzp,rkpq->rkzq/dot_general | solution.py:65
  145.6 0.1 eq.129
  145.7 7.9 %fusion.80 = f32[4,8192]{1,0:T(4,128)S(1)} fusion(f32[32,8,64,128]{3,2,1,0:T(8,128)} %fusion.79, s32[256]{0:T(256)S(1)} %eq.129), kind=kOutput, calls=%fused_computation.31.clone.1 | convolution fusion | flops 16778240 | bytes 8520704 | tf_op jit(solution)/shard_map/while/body/eval_jaxpr/dot_general | solution.py:75
  153.5 7.9 %fusion.81 = f32[4,8192]{1,0:T(4,128)S(1)} fusion(f32[4,8192]{1,0:T(4,128)S(1)} %fusion.80, f32[32,8,64,128]{3,2,1,0:T(8,128)} %fusion.79, f32[4,8192]{1,0:T(4,128)S(1)} %get-tuple-element.270, s32[256]{0:T(256)S(1)} %eq.129, pred[]{:T(512)S(6)} %compare.165), kind=kOutput, calls=%fused_computation.24.clone.1 | convolution fusion | flops 25265152 | bytes 8782849 | tf_op jit(solution)/shard_map/while/body/eval_jaxpr/dot_general | solution.py:76
  161.7 0.6 gather_fusion.3
  162.3 0.8 fusion.45
  163.1 8.4 %all-to-all-start = ((f32[8,64,128]{2,1,0:T(8,128)}), f32[8,64,128]{2,1,0:T(8,128)S(1)}, u32[]{:S(2)}, u32[]{:S(2)}) async-start(f32[8,64,128]{2,1,0:T(8,128)} %fusion.45), calls=%async_computation | async-start | bytes 524288 | tf_op jit(solution)/shard_map/all_to_all | solution.py:84
  171.6 9.9 %all-to-all-done = f32[8,64,128]{2,1,0:T(8,128)S(1)} async-done(((f32[8,64,128]{2,1,0:T(8,128)}), f32[8,64,128]{2,1,0:T(8,128)S(1)}, u32[]{:S(2)}, u32[]{:S(2)}) %all-to-all-start) | async-done | bytes 262176 | tf_op jit(solution)/shard_map/all_to_all | solution.py:84
  181.4 0.1 select_reduce_fusion
  181.6 0.6 gather_fusion.4
  182.2 0.7 broadcast_select_fusion
  182.9 3.6 %all-to-all-start.1 = ((bf16[8,64,128]{2,1,0:T(8,128)(2,1)}), bf16[8,64,128]{2,1,0:T(8,128)(2,1)S(1)}, u32[]{:S(2)}, u32[]{:S(2)}) async-start(bf16[8,64,128]{2,1,0:T(8,128)(2,1)} %broadcast_select_fusion), calls=%async_computation.1 | async-start | bytes 262144 | tf_op jit(solution)/shard_map/all_to_all | solution.py:91
  186.6 3.9 %slice.107 = f32[95,64,128]{2,1,0:T(8,128)} slice(f32[96,64,128]{2,1,0:T(8,128)} %get-tuple-element.149), slice={[0:95], [0:64], [0:128]} | slice | bytes 6225920 | tf_op jit(solution)/shard_map/slice | solution.py:120
  190.5 0.8 slice.106
  191.2 1.0 slice.108
  192.3 1.7 collective-permute-start.3
  194.0 3.6 %collective-permute-start.2 = (f32[1,64,128]{2,1,0:T(8,128)S(1)}, f32[1,64,128]{2,1,0:T(8,128)S(1)}, u32[]{:S(2)}, u32[]{:S(2)}) collective-permute-start(f32[1,64,128]{2,1,0:T(8,128)S(1)} %slice.106), channel_id=1, source_target_pairs={{0,1},{1,2},{2,3},{3,4},{4,5},{5,6},{6,7},{8,9},{9,10},{10,11},{11... | collective-permute-start | bytes 98312 | tf_op jit(solution)/shard_map/ppermute | solution.py:17
  197.7 58.0 %while.21 = (s32[]{:T(128)}, f32[3,32,64,128]{3,2,1,0:T(8,128)}, s32[3,32,8]{2,1,0:T(8,128)S(1)}, bf16[8,64,128]{2,1,0:T(8,128)(2,1)S(1)}, s32[3,32,8]{2,1,0:T(8...) while((s32[]{:T(128)}, f32[3,32,64,128]{3,2,1,0:T(8,128)}, s32[3,32,8]{2,1,0:T(8,128)S(1)}, ...), condition=%wide.region_8.10_spmd, body=%wide.region_7.9_spmd.sunk | while | flops 543168256 | bytes 38820436 | solution.py:104
  197.8 8.6 %gather_fusion = bf16[256,128,128]{2,1,0:T(8,128)(2,1)} fusion(bf16[32,128,128]{2,1,0:T(8,128)(2,1)S(1)} %get-tuple-element.304, s32[1024]{0:T(1024)S(1)} %pad_clamp_fusion.8), kind=kCustom, calls=%fused_computation.1.clone.clone.1 | custom fusion | bytes 16778240 | tf_op jit(solution)/shard_map/while/body/eval_jaxpr/jit(_take)/gather | solution.py:97
  206.4 0.1 reshape.423
  206.5 3.2 %gather_fusion.1 = bf16[256,64,128]{2,1,0:T(8,128)(2,1)} fusion(bf16[8,64,128]{2,1,0:T(8,128)(2,1)S(1)} %get-tuple-element.302, s32[1024]{0:T(1024)S(1)} %pad_clamp_fusion.9), kind=kCustom, calls=%fused_computation.2.clone.1 | custom fusion | bytes 8389632 | tf_op jit(solution)/shard_map/while/body/eval_jaxpr/jit(_take)/gather | solution.py:98
  209.7 7.3 %fusion.75 = f32[3,32,64,128]{3,2,1,0:T(8,128)} fusion(f32[3,32,64,128]{3,2,1,0:T(8,128)} %get-tuple-element.293, s32[]{:T(128)} %get-tuple-element.292, bf16[32,8,128,128]{3,2,1,0:T(8,128)(2,1)} %bitcast.104, pred[32,8]{1,0:T(8,128)(4,1)S(1)} %get-tuple-element.251, bf16[32,8,64,128]{3,2,1,0:T(8,128)(2,1)} %bitcast.105, ...), kind=kOutput, calls=%fused_computation.14.clone.1 | convolution fusion | flops 543162368 | bytes 13632512 | tf_op jit(solution)/shard_map/while/body/eval_jaxpr/rkzq,rkpq->rzp/dot_general | solution.py:101
  217.1 8.7 %gather_fusion = bf16[256,128,128]{2,1,0:T(8,128)(2,1)} fusion(bf16[32,128,128]{2,1,0:T(8,128)(2,1)S(1)} %get-tuple-element.304, s32[1024]{0:T(1024)S(1)} %pad_clamp_fusion.8), kind=kCustom, calls=%fused_computation.1.clone.clone.1 | custom fusion | bytes 16778240 | tf_op jit(solution)/shard_map/while/body/eval_jaxpr/jit(_take)/gather | solution.py:97
  225.7 0.1 reshape.423
  225.8 3.2 %gather_fusion.1 = bf16[256,64,128]{2,1,0:T(8,128)(2,1)} fusion(bf16[8,64,128]{2,1,0:T(8,128)(2,1)S(1)} %get-tuple-element.302, s32[1024]{0:T(1024)S(1)} %pad_clamp_fusion.9), kind=kCustom, calls=%fused_computation.2.clone.1 | custom fusion | bytes 8389632 | tf_op jit(solution)/shard_map/while/body/eval_jaxpr/jit(_take)/gather | solution.py:98
  229.0 7.3 %fusion.75 = f32[3,32,64,128]{3,2,1,0:T(8,128)} fusion(f32[3,32,64,128]{3,2,1,0:T(8,128)} %get-tuple-element.293, s32[]{:T(128)} %get-tuple-element.292, bf16[32,8,128,128]{3,2,1,0:T(8,128)(2,1)} %bitcast.104, pred[32,8]{1,0:T(8,128)(4,1)S(1)} %get-tuple-element.251, bf16[32,8,64,128]{3,2,1,0:T(8,128)(2,1)} %bitcast.105, ...), kind=kOutput, calls=%fused_computation.14.clone.1 | convolution fusion | flops 543162368 | bytes 13632512 | tf_op jit(solution)/shard_map/while/body/eval_jaxpr/rkzq,rkpq->rzp/dot_general | solution.py:101
  236.4 8.6 %gather_fusion = bf16[256,128,128]{2,1,0:T(8,128)(2,1)} fusion(bf16[32,128,128]{2,1,0:T(8,128)(2,1)S(1)} %get-tuple-element.304, s32[1024]{0:T(1024)S(1)} %pad_clamp_fusion.8), kind=kCustom, calls=%fused_computation.1.clone.clone.1 | custom fusion | bytes 16778240 | tf_op jit(solution)/shard_map/while/body/eval_jaxpr/jit(_take)/gather | solution.py:97
  245.1 0.1 reshape.423
  245.2 3.2 %gather_fusion.1 = bf16[256,64,128]{2,1,0:T(8,128)(2,1)} fusion(bf16[8,64,128]{2,1,0:T(8,128)(2,1)S(1)} %get-tuple-element.302, s32[1024]{0:T(1024)S(1)} %pad_clamp_fusion.9), kind=kCustom, calls=%fused_computation.2.clone.1 | custom fusion | bytes 8389632 | tf_op jit(solution)/shard_map/while/body/eval_jaxpr/jit(_take)/gather | solution.py:98
  248.3 7.3 %fusion.75 = f32[3,32,64,128]{3,2,1,0:T(8,128)} fusion(f32[3,32,64,128]{3,2,1,0:T(8,128)} %get-tuple-element.293, s32[]{:T(128)} %get-tuple-element.292, bf16[32,8,128,128]{3,2,1,0:T(8,128)(2,1)} %bitcast.104, pred[32,8]{1,0:T(8,128)(4,1)S(1)} %get-tuple-element.251, bf16[32,8,64,128]{3,2,1,0:T(8,128)(2,1)} %bitcast.105, ...), kind=kOutput, calls=%fused_computation.14.clone.1 | convolution fusion | flops 543162368 | bytes 13632512 | tf_op jit(solution)/shard_map/while/body/eval_jaxpr/rkzq,rkpq->rzp/dot_general | solution.py:101
  255.7 12.6 %fusion.44 = f32[96,64,128]{2,1,0:T(8,128)} fusion(f32[96,64,128]{2,1,0:T(8,128)} %param.13, f32[96,64,128]{2,1,0:T(8,128)} %get-tuple-element.149, f32[95,64,128]{2,1,0:T(8,128)} %slice.107, f32[1,64,128]{2,1,0:T(8,128)S(1)} %collective-permute-done.2, f32[96,64,128]{2,1,0:T(8,128)} %get-tuple-element.148, f32[96,63,128]{2,1,0:T(8,128)} %bitcast.106, ...), kind=kLoop, calls=%fused_computation.55 | loop fusion | flops 8650752 | bytes 28286976 | tf_op jit(solution)/shard_map/max | solution.py:126
  (61 shorter events, 0.9 us)
Async XLA Ops:
  1.0 50.5 %collective-permute-start.1 = (f32[96,1,128]{2,1,0:T(1,128)S(1)}, f32[96,1,128]{2,1,0:T(1,128)S(1)}, u32[]{:S(2)}, u32[]{:S(2)}) collective-permute-start(f32[96,1,128]{2,1,0:T(1,128)S(1)} %slice.36), channel_id=1, source_target_pairs={{8,0},{16,8},{24,16},{9,1},{17,9},{25,17},{10,2},{18,10},{26,18},{... | collective-permute-start | bytes 147464 | tf_op jit(solution)/shard_map/ppermute | solution.py:17
  3.1 48.5 %collective-permute-start = (f32[1,64,128]{2,1,0:T(8,128)S(1)}, f32[1,64,128]{2,1,0:T(8,128)S(1)}, u32[]{:S(2)}, u32[]{:S(2)}) collective-permute-start(f32[1,64,128]{2,1,0:T(8,128)S(1)} %slice.34), channel_id=1, source_target_pairs={{1,0},{2,1},{3,2},{4,3},{5,4},{6,5},{7,6},{9,8},{10,9},{11,10},{12... | collective-permute-start | bytes 98312 | tf_op jit(solution)/shard_map/ppermute | solution.py:17
  4.4 5.6 %copy-start.2 = (s32[16]{0:T(128)S(1)}, s32[16]{0:T(128)}, u32[]{:S(2)}) copy-start(s32[16]{0:T(128)} %param.17) | copy-start | bytes 196
  4.4 6.3 %copy-start.5 = (s32[768,8]{0,1:T(8,128)S(1)}, s32[768,8]{0,1:T(8,128)}, u32[]{:S(2)}) copy-start(s32[768,8]{0,1:T(8,128)} %param.16) | copy-start | bytes 73732
  4.4 42.9 %copy-start.1 = (f32[96,64,128]{2,1,0:T(8,128)S(1)}, f32[96,64,128]{2,1,0:T(8,128)}, u32[]{:S(2)}) copy-start(f32[96,64,128]{2,1,0:T(8,128)} %param.13) | copy-start | bytes 9437188
  49.5 1.9 copy-start.6
  51.5 10.9 %copy-start = (bf16[32,128,128]{2,1,0:T(8,128)(2,1)S(1)}, bf16[32,128,128]{2,1,0:T(8,128)(2,1)}, u32[]{:S(2)}) copy-start(bf16[32,128,128]{2,1,0:T(8,128)(2,1)} %param.14) | copy-start | bytes 3145732
  161.6 19.9 %copy-start.3 = (f32[2,64,128]{2,1,0:T(8,128)S(1)}, f32[2,64,128]{2,1,0:T(8,128)}, u32[]{:S(2)}) copy-start(f32[2,64,128]{2,1,0:T(8,128)} %param.19) | copy-start | bytes 196612
  161.7 19.9 %copy-start.4 = (f32[2,64,128]{2,1,0:T(8,128)S(1)}, f32[2,64,128]{2,1,0:T(8,128)}, u32[]{:S(2)}) copy-start(f32[2,64,128]{2,1,0:T(8,128)} %param.18) | copy-start | bytes 196612
  163.1 18.3 %all-to-all-start = ((f32[8,64,128]{2,1,0:T(8,128)}), f32[8,64,128]{2,1,0:T(8,128)S(1)}, u32[]{:S(2)}, u32[]{:S(2)}) async-start(f32[8,64,128]{2,1,0:T(8,128)} %fusion.45), calls=%async_computation | async-start | bytes 524288 | tf_op jit(solution)/shard_map/all_to_all | solution.py:84
  182.9 14.8 %all-to-all-start.1 = ((bf16[8,64,128]{2,1,0:T(8,128)(2,1)}), bf16[8,64,128]{2,1,0:T(8,128)(2,1)S(1)}, u32[]{:S(2)}, u32[]{:S(2)}) async-start(bf16[8,64,128]{2,1,0:T(8,128)(2,1)} %broadcast_select_fusion), calls=%async_computation.1 | async-start | bytes 262144 | tf_op jit(solution)/shard_map/all_to_all | solution.py:91
  192.3 63.4 %collective-permute-start.3 = (f32[96,1,128]{2,1,0:T(1,128)S(1)}, f32[96,1,128]{2,1,0:T(1,128)S(1)}, u32[]{:S(2)}, u32[]{:S(2)}) collective-permute-start(f32[96,1,128]{2,1,0:T(1,128)S(1)} %slice.108), channel_id=1, source_target_pairs={{0,8},{8,16},{16,24},{1,9},{9,17},{17,25},{2,10},{10,18},{18,26},{... | collective-permute-start | bytes 147464 | tf_op jit(solution)/shard_map/ppermute | solution.py:17
  194.0 61.7 %collective-permute-start.2 = (f32[1,64,128]{2,1,0:T(8,128)S(1)}, f32[1,64,128]{2,1,0:T(8,128)S(1)}, u32[]{:S(2)}, u32[]{:S(2)}) collective-permute-start(f32[1,64,128]{2,1,0:T(8,128)S(1)} %slice.106), channel_id=1, source_target_pairs={{0,1},{1,2},{2,3},{3,4},{4,5},{5,6},{6,7},{8,9},{9,10},{10,11},{11... | collective-permute-start | bytes 98312 | tf_op jit(solution)/shard_map/ppermute | solution.py:17
where the time goes:
time: 271 us; the launch traced here: 268 us
  matrix products  94.2 us (35%)
  local copies, waits for them, and re-layouts  77.1 us (28%)
  other arithmetic  66.5 us (25%)
  starting transfers between devices  20 us (7%)
  waiting for transfers between devices  9.87 us (4%)
    gather x3, local copies, waits for them, and re-layouts, project(): stencil = jnp.take(footprints, offsets, axis=0)  26 us
    gather x3, local copies, waits for them, and re-layouts, backproject(): stencil = jnp.take(footprints, offsets, axis=0)  25.9 us
    dot_general x3, matrix products, project(): jnp.einsum('rzp,rkpq->rkzq', pixels, stencil, preferred_element_type=jnp....  25 us
    dot_general x3, matrix products, project(): lax.dot_general(selector, low, dims, preferred_element_type=jnp.float32)  23.8 us
    dot_general x3, matrix products, project(): lax.dot_general(selector, high, dims, preferred_element_type=jnp.float32)  23.6 us
    dot_general x3, matrix products, backproject(): jnp.einsum('rkzq,rkpq->rzp', values, stencil, preferred_element_type=jnp....  21.8 us
    select_n x1, other arithmetic, per_device(): compact_targets = jnp.take(rank, targets, axis=0)  15.1 us
    max x1, other arithmetic, per_device(): return jnp.maximum(updated, 0.0)  12.6 us
  transfers between devices with their start and end apart: 6, of which 1 were waited for; matrix products, arithmetic and copies ran while one was open for 42% of the time, Pallas kernels for 0%

commit v1 on v0

v1 whole, which is shorter than its diff:
```python
import functools
import math

import jax
import jax.numpy as jnp
from jax import lax
from jax.experimental import pallas as pl
from jax.experimental.pallas import tpu as pltpu
from jax.sharding import PartitionSpec as P

smoothing = 0.04
step_length = 2.0
variation_weight = 1.0

SUB = 8
WIDE = 256
WIRE = jnp.float32
VMEM_LIMIT = 56 * 2**20
MESH = pl.DeviceIdType.MESH
F32 = jnp.float32
BF16 = jnp.bfloat16


def iota(shape, axis):
    return lax.broadcasted_iota(jnp.int32, shape, axis)


def repeat_rows(x):
    rows, cols = x.shape
    tall = jnp.broadcast_to(x[:, None, :], (rows, SUB, cols)).reshape(rows * SUB, cols)
    keep = (iota(tall.shape, 0) & (SUB - 1)) == (iota(tall.shape, 1) & (SUB - 1))
    return jnp.where(keep, tall, 0.0).astype(BF16)


def dot(a, b):
    return lax.dot_general(a, b, (((1,), (0,)), ((), ())), preferred_element_type=F32)


def exchange_kernel(
    touch, owners, slabs, early,
    vol_ref, table_ref, index_ref, block_ref, slot_ref, meas_ref, wt_ref,
    base_out, back_out, resid_ref,
    vv, vb, fwd, bwd, base, edge_lo, edge_hi, next_z, prev_z, prev_flux,
    send, recv, back_send, back_recv,
    load_sem, out_sem, halo_send, halo_recv, part_send, part_recv, res_send, res_recv,
):
    rows, slices, px = vol_ref.shape
    rays = table_ref.shape[1]
    nfoot = table_ref.shape[0] // px
    crossings, all_rows = block_ref.shape
    owned = meas_ref.shape[0]
    keys = nfoot * touch
    zt = slices // SUB
    ts = touch * SUB
    pos = lax.axis_index("tile")
    layer = lax.axis_index("slab")
    t_next, t_prev = lax.rem(pos + 1, owners), lax.rem(pos + owners - 1, owners)
    z_next, z_prev = lax.rem(layer + 1, slabs), lax.rem(layer + slabs - 1, slabs)

    barrier = pltpu.get_barrier_semaphore()
    peers = [(layer, lax.rem(pos + d, owners)) for d in range(1, owners)]
    peers += [(z_next, pos), (z_prev, pos), (z_next, t_prev), (z_prev, t_next)]
    for peer in peers:
        pl.semaphore_signal(barrier, inc=1, device_id=peer, device_id_type=MESH)

    parts = 4
    piece = rows // parts
    loads = [
        pltpu.make_async_copy(
            vol_ref.at[pl.ds(c * piece, piece)], vv.at[pl.ds(1 + c * piece, piece)], load_sem.at[c]
        )
        for c in range(parts)
    ]
    for copy in loads:
        copy.start()

    blocks = block_ref[...]
    slot = jnp.zeros_like(blocks)
    for b in range(slot_ref.shape[0]):
        slot = jnp.where(blocks == b, slot_ref[b], slot)
    owner = slot >> (owned.bit_length() - 1) if owned & (owned - 1) == 0 else slot // owned
    local = jnp.where(owner == pos, slot - pos * owned, 0).astype(F32)
    locals_ = [
        jnp.max(local[:, n * rows : (n + 1) * rows], axis=(0, 1), keepdims=True)
        for n in range(owners)
    ]
    mine = (iota((all_rows, rows), 0) == iota((all_rows, rows), 1) + pos * rows).astype(BF16)
    my_owner = dot(owner.astype(BF16), mine)
    rank = jnp.zeros((1, 1), F32)
    compact = jnp.zeros_like(my_owner)
    place = []
    for o in range(owners):
        here = my_owner == o
        found = jnp.max(jnp.where(here, 1.0, 0.0), axis=(0, 1), keepdims=True)
        place.append([jnp.where(rank == t, found, 0.0) for t in range(touch)])
        compact = jnp.where(here, rank, compact)
        rank = rank + found
    key = index_ref[...] * touch + compact.astype(jnp.int32)
    ids = iota((keys, rows), 0)
    count = jnp.zeros((keys, rows), F32)
    for k in range(crossings):
        count = count + jnp.where(ids == key[k : k + 1, :], 1.0, 0.0)
    widen = (iota((rows, rows * SUB), 1) // SUB == iota((rows, rows * SUB), 0)).astype(BF16)
    spread = dot(count.astype(BF16), widen)
    step = WIDE // SUB
    for c in range(keys // step):
        fwd[c * WIDE : (c + 1) * WIDE, :] = repeat_rows(spread[c * step : (c + 1) * step])

    pl.semaphore_wait(barrier, len(peers))

    def remote(src, dst, sem_s, sem_r, peer):
        return pltpu.make_async_remote_copy(
            src_ref=src, dst_ref=dst, send_sem=sem_s, recv_sem=sem_r,
            device_id=peer, device_id_type=MESH,
        )

    def halo(i, src, dst, peer):
        return remote(src, dst, halo_send.at[i], halo_recv.at[i], peer)

    halos = [
        halo(0, vol_ref.at[pl.ds(0, 1)], vv.at[pl.ds(rows + 1, 1)], (layer, t_prev)),
        halo(1, vol_ref.at[pl.ds(rows - 1, 1)], vv.at[pl.ds(0, 1)], (layer, t_next)),
    ]
    for copy in halos:
        copy.start()

    for c in range(parts):
        loads[c].wait()
        for z in range(zt):
            part = vv[1 + c * piece : 1 + (c + 1) * piece, z * SUB : (z + 1) * SUB, :]
            vb[c * piece * SUB : (c + 1) * piece * SUB, z * px : (z + 1) * px] = part.reshape(
                piece * SUB, px
            ).astype(BF16)
    edge_lo[...] = vv[1 : rows + 1, 0, :]
    edge_hi[...] = vv[1 : rows + 1, slices - 1, :]
    more = [
        halo(2, edge_lo, next_z.at[pl.ds(0, rows)], (z_prev, pos)),
        halo(3, edge_hi, prev_z.at[pl.ds(0, rows)], (z_next, pos)),
        halo(4, edge_hi.at[pl.ds(0, SUB)], prev_z.at[pl.ds(rows, SUB)], (z_next, t_prev)),
        halo(5, edge_lo.at[pl.ds(rows - SUB, SUB)], next_z.at[pl.ds(rows, SUB)], (z_prev, t_next)),
    ]
    for copy in more:
        copy.start()
    halos += more

    per = WIDE // ts
    total = jnp.zeros((zt * ts, rays), F32)
    for c in range(nfoot // per):
        summed = dot(fwd[c * WIDE : (c + 1) * WIDE, :], vb[...])
        turned = jnp.concatenate(
            [
                jnp.concatenate(
                    [summed[f * ts : (f + 1) * ts, z * px : (z + 1) * px] for z in range(zt)], axis=0
                )
                for f in range(per)
            ],
            axis=1,
        ).astype(BF16)
        total = total + dot(turned, table_ref[c * per * px : (c + 1) * per * px, :])
    total = total.reshape(zt, touch, SUB, rays)
    partial = [total[:, t].reshape(slices, rays) for t in range(touch)]
    for o in range(owners):
        send[o] = sum(place[o][t] * partial[t] for t in range(touch)).astype(WIRE)

    there = []
    for d in range(1, owners):
        peer = lax.rem(pos + d, owners)
        there.append(
            remote(send.at[peer], recv.at[pos], part_send.at[d], part_recv.at[d], (layer, peer))
        )
    for copy in there:
        copy.start()
    recv[pl.ds(pos, 1)] = send[pl.ds(pos, 1)]

    for copy in halos:
        copy.wait_recv()
    last_row = pos == owners - 1
    last_slice = layer == slabs - 1
    sub = iota((slices, px), 0)
    lane = iota((slices, px), 1)

    def inverse(a, b, c):
        return lax.rsqrt(a * a + b * b + c * c + smoothing)

    def column(v, where):
        return jnp.where(where == px - 1, 0.0, pltpu.roll(v, px - 1, 1) - v)

    lower = prev_z[0:rows, :]
    g_z = edge_lo[...] - lower
    after = iota((rows, px), 0)
    below = pltpu.roll(lower, rows - 1, 0)
    below = jnp.where(after == rows - 1, prev_z[rows : rows + 1, :], below)
    g_r = jnp.where(jnp.logical_and(after == rows - 1, last_row), 0.0, below - lower)
    flux = g_z * inverse(g_r, g_z, column(lower, iota((rows, px), 1)))
    prev_flux[...] = jnp.where(layer == 0, 0.0, flux)

    def next_slice(v, edge):
        moved = jnp.where(sub == slices - 1, edge, pltpu.roll(v, slices - 1, 0)) - v
        return jnp.where(jnp.logical_and(sub == slices - 1, last_slice), 0.0, moved)

    before = vv[0]
    g_r = vv[1] - before
    g_z = next_slice(before, next_z[rows + SUB - 1 : rows + SUB, :])
    flux = g_r * inverse(g_r, g_z, column(before, lane))
    flux = jnp.where(pos == 0, 0.0, flux)

    def tv_row(r, flux):
        v = vv[r + 1]
        g_r = vv[r + 2] - v
        g_r = jnp.where(jnp.logical_and(r == rows - 1, last_row), 0.0, g_r)
        g_z = next_slice(v, next_z[pl.ds(r, 1), :])
        g_c = column(v, lane)
        inv = inverse(g_r, g_z, g_c)
        f_r, f_z, f_c = g_r * inv, g_z * inv, g_c * inv
        came = jnp.where(sub == 0, prev_flux[pl.ds(r, 1), :], pltpu.roll(f_z, 1, 0))
        variation = (flux - f_r) + (came - f_z) + (pltpu.roll(f_c, 1, 1) - f_c)
        base[r] = v - (step_length * variation_weight) * variation
        return f_r

    flux = lax.fori_loop(0, early, tv_row, flux)

    for copy in there:
        copy.wait_recv()
    residual = []
    for l in range(owned):
        own = sum(
            jnp.where(locals_[n] == l, 1.0, 0.0) * recv[n].astype(F32) for n in range(owners)
        )
        residual.append((wt_ref[l] * (own - meas_ref[l])).astype(BF16).astype(F32))
    for n in range(owners):
        picked = sum(jnp.where(locals_[n] == l, 1.0, 0.0) * residual[l] for l in range(owned))
        back_send[n] = picked.astype(BF16)
    home = []
    for d in range(1, owners):
        peer = lax.rem(pos + d, owners)
        home.append(
            remote(
                back_send.at[peer], back_recv.at[pos], res_send.at[d], res_recv.at[d], (layer, peer)
            )
        )
    for copy in home:
        copy.start()
    back_recv[pl.ds(pos, 1)] = back_send[pl.ds(pos, 1)]

    lax.fori_loop(early, rows, tv_row, flux)
    write_base = pltpu.make_async_copy(base, base_out, out_sem.at[0])
    write_base.start()

    widen = (iota((keys, keys * SUB), 1) // SUB == iota((keys, keys * SUB), 0)).astype(BF16)
    spread = dot(count.T.astype(BF16), widen)
    step = math.gcd(rows, 16)
    for c in range(rows // step):
        bwd[c * step * SUB : (c + 1) * step * SUB, :] = repeat_rows(
            spread[c * step : (c + 1) * step]
        )
    write_back = pltpu.make_async_copy(bwd, back_out, out_sem.at[1])
    write_back.start()

    for copy in home:
        copy.wait_recv()
    arrived = []
    for t in range(touch):
        one = sum(place[o][t] * back_recv[o].astype(F32) for o in range(owners))
        arrived.append(one.reshape(zt, SUB, rays))
    resid_ref[...] = jnp.stack(arrived, axis=1).reshape(zt * ts, rays).astype(BF16)
    write_base.wait()
    write_back.wait()
    for copy in halos + there + home:
        copy.wait_send()


def update_kernel(touch, resid_ref, table_ref, back_ref, base_ref, out_ref, grads):
    rows, slices, px = base_ref.shape
    nfoot = table_ref.shape[0] // px
    zt = slices // SUB
    ts = touch * SUB

    @pl.when(pl.program_id(0) == 0)
    def _():
        per = WIDE // px
        for c in range(nfoot // per):
            piece = lax.dot_general(
                resid_ref[...],
                table_ref[c * WIDE : (c + 1) * WIDE, :],
                (((1,), (1,)), ((), ())),
                preferred_element_type=F32,
            )
            for f in range(per):
                for z in range(zt):
                    at = (c * per + f) * ts
                    grads[at : at + ts, z * px : (z + 1) * px] = piece[
                        z * ts : (z + 1) * ts, f * px : (f + 1) * px
                    ].astype(BF16)

    grad = dot(back_ref[...], grads[...])
    for z in range(zt):
        at = slice(z * SUB, (z + 1) * SUB)
        one = grad[:, z * px : (z + 1) * px].reshape(rows, SUB, px)
        out_ref[:, at, :] = jnp.maximum(base_ref[:, at, :] - step_length * one, 0.0)


def per_device(owners, slabs, volume, footprints, foot_index, ray_block, ray_slot, measured, weights):
    rows, slices, px = volume.shape
    nfoot, _, rays = footprints.shape
    touch = owners // 2
    keys = nfoot * touch
    zt = slices // SUB
    table = footprints.reshape(nfoot * px, rays)
    any_space = pl.BlockSpec(memory_space=pl.ANY)
    vmem = pl.BlockSpec(memory_space=pltpu.VMEM)
    smem = pl.BlockSpec(memory_space=pltpu.SMEM)
    dma = pltpu.SemaphoreType.DMA
    base, back, resid = pl.pallas_call(
        functools.partial(exchange_kernel, touch, owners, slabs, rows // 2),
        out_shape=(
            jax.ShapeDtypeStruct(volume.shape, F32),
            jax.ShapeDtypeStruct((rows * SUB, keys * SUB), BF16),
            jax.ShapeDtypeStruct((zt * touch * SUB, rays), BF16),
        ),
        in_specs=[any_space, vmem, vmem, vmem, smem, vmem, vmem],
        out_specs=(any_space, any_space, vmem),
        scratch_shapes=[
            pltpu.VMEM((rows + 2, slices, px), F32),
            pltpu.VMEM((rows * SUB, zt * px), BF16),
            pltpu.VMEM((keys * SUB, rows * SUB), BF16),
            pltpu.VMEM((rows * SUB, keys * SUB), BF16),
            pltpu.VMEM((rows, slices, px), F32),
            pltpu.VMEM((rows, px), F32),
            pltpu.VMEM((rows, px), F32),
            pltpu.VMEM((rows + SUB, px), F32),
            pltpu.VMEM((rows + SUB, px), F32),
            pltpu.VMEM((rows, px), F32),
            pltpu.VMEM((owners, slices, rays), WIRE),
            pltpu.VMEM((owners, slices, rays), WIRE),
            pltpu.VMEM((owners, slices, rays), BF16),
            pltpu.VMEM((owners, slices, rays), BF16),
            dma((4,)),
            dma((2,)),
            dma((6,)),
            dma((6,)),
            dma((owners,)),
            dma((owners,)),
            dma((owners,)),
            dma((owners,)),
        ],
        compiler_params=pltpu.CompilerParams(
            collective_id=0, has_side_effects=True, vmem_limit_bytes=VMEM_LIMIT
        ),
    )(volume, table, foot_index.T, ray_block.T, ray_slot, measured, weights)
    steps = 4
    some = rows // steps
    return pl.pallas_call(
        functools.partial(update_kernel, touch),
        grid=(steps,),
        out_shape=jax.ShapeDtypeStruct(volume.shape, F32),
        in_specs=[
            pl.BlockSpec(resid.shape, lambda i: (0, 0)),
            pl.BlockSpec(table.shape, lambda i: (0, 0)),
            pl.BlockSpec((some * SUB, keys * SUB), lambda i: (i, 0)),
            pl.BlockSpec((some, slices, px), lambda i: (i, 0, 0)),
        ],
        out_specs=pl.BlockSpec((some, slices, px), lambda i: (i, 0, 0)),
        scratch_shapes=[pltpu.VMEM((keys * SUB, zt * px), BF16)],
        compiler_params=pltpu.CompilerParams(vmem_limit_bytes=VMEM_LIMIT),
    )(resid, table, back, base)


def solution(mesh):
    in_specs = (
        P("tile", "slab", None),
        P(),
        P("tile", None),
        P(),
        P(),
        P("tile", "slab", None),
        P("tile", "slab", None),
    )
    out_specs = P("tile", "slab", None)
    body = functools.partial(per_device, mesh.shape["tile"], mesh.shape["slab"])
    return jax.shard_map(body, mesh=mesh, in_specs=in_specs, out_specs=out_specs, check_vma=False)
```

time: 271 us -> 37.5 us (0.14)
  the two profiles are of different devices: /device:TPU:0 before, /device:TPU:1 now
where the time goes in v1:
time: 37.5 us; the launch traced here: 37.3 us
  Pallas kernels  37.3 us (99%)
    pallas_call x1, Pallas kernels, per_device(): pl.pallas_call(functools.partial(exchange_kernel, touch, owners, slabs, r...  30.5 us
    pallas_call x1, Pallas kernels, per_device(): pl.pallas_call(functools.partial(update_kernel, touch), grid=(steps,), ou...  6.81 us

profile of v1, /device:TPU:1, one launch (start us, length us, event | category | flops | bytes accessed | tf_op | source)
XLA Modules:
  0.0 37.3 jit_solution(8033714327369552768)
XLA Ops:
  0.0 30.5 %shard_map.73 = (f32[96,64,128]{2,1,0:T(8,128)}, bf16[768,1024]{1,0:T(8,128)(2,1)}, bf16[256,128]{1,0:T(8,128)(2,1)}) custom-call(f32[96,64,128]{2,1,0:T(8,128)} %vol_ref.1, bf16[4096,128]{1,0:T(8,128)(2,1)} %bitcast.3, s32[8,96]{1,0:T(8,128)} %bitcast.6, s32[8,768]{1,0:T(8,128)} %bitcast.5, s32[16]{0:T(128)} %slot_ref.1, f32[2,64,128]{2,1,0:T(8,128)} %meas_ref.1, ...), custom_call_target="tpu_custom_call" | custom-call | tf_op jit(solution)/shard_map/pallas_call | solution.py:313
  30.5 6.8 %shard_map.74 = f32[96,64,128]{2,1,0:T(8,128)} custom-call(bf16[256,128]{1,0:T(8,128)(2,1)} %get-tuple-element.8.resid_ref, bf16[4096,128]{1,0:T(8,128)(2,1)} %bitcast.4, bf16[768,1024]{1,0:T(8,128)(2,1)} %get-tuple-element.9.back_ref, f32[96,64,128]{2,1,0:T(8,128)} %get-tuple-element.10.base_ref), custom_call_target="tpu_custom_call" | custom-call | tf_op jit(solution)/shard_map/pallas_call | solution.py:352

commit v2 on v1

--- a/solution.py
+++ b/solution.py
@@ -14,8 +14,9 @@
 
 SUB = 8
 WIDE = 256
-WIRE = jnp.float32
+WIRE = jnp.bfloat16
 VMEM_LIMIT = 56 * 2**20
+TOGETHER = 4
 MESH = pl.DeviceIdType.MESH
 F32 = jnp.float32
 BF16 = jnp.bfloat16
@@ -38,9 +39,9 @@
 
 def exchange_kernel(
     touch, owners, slabs, early,
-    vol_ref, table_ref, index_ref, block_ref, slot_ref, meas_ref, wt_ref,
+    vol_ref, table_hbm, index_ref, block_ref, slot_ref, meas_ref, wt_ref,
     base_out, back_out, resid_ref,
-    vv, vb, fwd, bwd, base, edge_lo, edge_hi, next_z, prev_z, prev_flux,
+    table_ref, vv, vb, fwd, bwd, base, edge_lo, edge_hi, next_z, prev_z, prev_flux, upper,
     send, recv, back_send, back_recv,
     load_sem, out_sem, halo_send, halo_recv, part_send, part_recv, res_send, res_recv,
 ):
@@ -73,6 +74,8 @@
     ]
     for copy in loads:
         copy.start()
+    load_table = pltpu.make_async_copy(table_hbm, table_ref, load_sem.at[parts])
+    load_table.start()
 
     blocks = block_ref[...]
     slot = jnp.zeros_like(blocks)
@@ -143,6 +146,8 @@
         copy.start()
     halos += more
 
+    load_table.wait()
+
     per = WIDE // ts
     total = jnp.zeros((zt * ts, rays), F32)
     for c in range(nfoot // per):
@@ -172,12 +177,11 @@
         copy.start()
     recv[pl.ds(pos, 1)] = send[pl.ds(pos, 1)]
 
-    for copy in halos:
-        copy.wait_recv()
     last_row = pos == owners - 1
     last_slice = layer == slabs - 1
     sub = iota((slices, px), 0)
     lane = iota((slices, px), 1)
+    after = iota((rows, px), 0)
 
     def inverse(a, b, c):
         return lax.rsqrt(a * a + b * b + c * c + smoothing)
@@ -185,30 +189,21 @@
     def column(v, where):
         return jnp.where(where == px - 1, 0.0, pltpu.roll(v, px - 1, 1) - v)
 
-    lower = prev_z[0:rows, :]
-    g_z = edge_lo[...] - lower
-    after = iota((rows, px), 0)
-    below = pltpu.roll(lower, rows - 1, 0)
-    below = jnp.where(after == rows - 1, prev_z[rows : rows + 1, :], below)
-    g_r = jnp.where(jnp.logical_and(after == rows - 1, last_row), 0.0, below - lower)
-    flux = g_z * inverse(g_r, g_z, column(lower, iota((rows, px), 1)))
-    prev_flux[...] = jnp.where(layer == 0, 0.0, flux)
+    def slice_flux(corner):
+        lower = prev_z[0:rows, :]
+        g_z = edge_lo[...] - lower
+        below = pltpu.roll(lower, rows - 1, 0)
+        if corner is not None:
+            below = jnp.where(after == rows - 1, jnp.where(last_row, lower, corner), below)
+        flux = g_z * inverse(below - lower, g_z, column(lower, iota((rows, px), 1)))
+        prev_flux[...] = jnp.where(layer == 0, 0.0, flux)
 
     def next_slice(v, edge):
-        moved = jnp.where(sub == slices - 1, edge, pltpu.roll(v, slices - 1, 0)) - v
-        return jnp.where(jnp.logical_and(sub == slices - 1, last_slice), 0.0, moved)
-
-    before = vv[0]
-    g_r = vv[1] - before
-    g_z = next_slice(before, next_z[rows + SUB - 1 : rows + SUB, :])
-    flux = g_r * inverse(g_r, g_z, column(before, lane))
-    flux = jnp.where(pos == 0, 0.0, flux)
-
-    def tv_row(r, flux):
-        v = vv[r + 1]
-        g_r = vv[r + 2] - v
-        g_r = jnp.where(jnp.logical_and(r == rows - 1, last_row), 0.0, g_r)
-        g_z = next_slice(v, next_z[pl.ds(r, 1), :])
+        return jnp.where(sub == slices - 1, edge, pltpu.roll(v, slices - 1, 0)) - v
+
+    def tv_row(r, flux, v, below):
+        g_r = below - v
+        g_z = next_slice(v, upper[pl.ds(r, 1), :])
         g_c = column(v, lane)
         inv = inverse(g_r, g_z, g_c)
         f_r, f_z, f_c = g_r * inv, g_z * inv, g_c * inv
@@ -217,7 +212,22 @@
         base[r] = v - (step_length * variation_weight) * variation
         return f_r
 
-    flux = lax.fori_loop(0, early, tv_row, flux)
+    def tv_rows(first, flux, final=False):
+        for j in range(TOGETHER):
+            v, below = vv[first + j + 1], vv[first + j + 2]
+            if final and j == TOGETHER - 1:
+                below = jnp.where(last_row, v, below)
+            flux = tv_row(first + j, flux, v, below)
+        return flux
+
+    def tv_step(i, flux):
+        return tv_rows(i * TOGETHER, flux)
+
+    for copy in halos[2:4]:
+        copy.wait_recv()
+    upper[...] = jnp.where(last_slice, edge_hi[...], next_z[0:rows, :])
+    slice_flux(None)
+    flux = lax.fori_loop(0, early, tv_step, jnp.zeros((slices, px), F32))
 
     for copy in there:
         copy.wait_recv()
@@ -242,7 +252,17 @@
         copy.start()
     back_recv[pl.ds(pos, 1)] = back_send[pl.ds(pos, 1)]
 
-    lax.fori_loop(early, rows, tv_row, flux)
+    for copy in halos[:2] + halos[4:]:
+        copy.wait_recv()
+    slice_flux(prev_z[rows : rows + 1, :])
+    before = vv[0]
+    corner = jnp.where(last_slice, before[slices - 1 : slices, :], next_z[rows + SUB - 1 : rows + SUB, :])
+    g_r = vv[1] - before
+    came = g_r * inverse(g_r, next_slice(before, corner), column(before, lane))
+    base[0] = base[0] - (step_length * variation_weight) * jnp.where(pos == 0, 0.0, came)
+    steps = rows // TOGETHER
+    flux = lax.fori_loop(early, steps - 1, tv_step, flux)
+    tv_rows((steps - 1) * TOGETHER, flux, True)
     write_base = pltpu.make_async_copy(base, base_out, out_sem.at[0])
     write_base.start()
 
@@ -311,15 +331,16 @@
     smem = pl.BlockSpec(memory_space=pltpu.SMEM)
     dma = pltpu.SemaphoreType.DMA
     base, back, resid = pl.pallas_call(
-        functools.partial(exchange_kernel, touch, owners, slabs, rows // 2),
+        functools.partial(exchange_kernel, touch, owners, slabs, rows // TOGETHER // 2),
         out_shape=(
             jax.ShapeDtypeStruct(volume.shape, F32),
             jax.ShapeDtypeStruct((rows * SUB, keys * SUB), BF16),
             jax.ShapeDtypeStruct((zt * touch * SUB, rays), BF16),
         ),
-        in_specs=[any_space, vmem, vmem, vmem, smem, vmem, vmem],
+        in_specs=[any_space, any_space, vmem, vmem, smem, vmem, vmem],
         out_specs=(any_space, any_space, vmem),
         scratch_shapes=[
+            pltpu.VMEM(table.shape, BF16),
             pltpu.VMEM((rows + 2, slices, px), F32),
             pltpu.VMEM((rows * SUB, zt * px), BF16),
             pltpu.VMEM((keys * SUB, rows * SUB), BF16),
@@ -330,11 +351,12 @@
             pltpu.VMEM((rows + SUB, px), F32),
             pltpu.VMEM((rows + SUB, px), F32),
             pltpu.VMEM((rows, px), F32),
+            pltpu.VMEM((rows, px), F32),
             pltpu.VMEM((owners, slices, rays), WIRE),
             pltpu.VMEM((owners, slices, rays), WIRE),
             pltpu.VMEM((owners, slices, rays), BF16),
             pltpu.VMEM((owners, slices, rays), BF16),
-            dma((4,)),
+            dma((5,)),
             dma((2,)),
             dma((6,)),
             dma((6,)),

time: 37.5 us -> 28.1 us (0.75)
  the two profiles are of different devices: /device:TPU:1 before, /device:TPU:0 now
where the time goes in v2:
time: 28.1 us; the launch traced here: 27.9 us
  Pallas kernels  27.9 us (99%)
    pallas_call x1, Pallas kernels, per_device(): pl.pallas_call(functools.partial(exchange_kernel, touch, owners, slabs, r...  21.1 us
    pallas_call x1, Pallas kernels, per_device(): pl.pallas_call(functools.partial(update_kernel, touch), grid=(steps,), ou...  6.81 us

profile of v2, /device:TPU:0, one launch (start us, length us, event | category | flops | bytes accessed | tf_op | source)
XLA Modules:
  0.0 27.9 jit_solution(6125432682646833060)
XLA Ops:
  0.0 21.1 %shard_map.73 = (f32[96,64,128]{2,1,0:T(8,128)}, bf16[768,1024]{1,0:T(8,128)(2,1)}, bf16[256,128]{1,0:T(8,128)(2,1)}) custom-call(f32[96,64,128]{2,1,0:T(8,128)} %vol_ref.1, bf16[4096,128]{1,0:T(8,128)(2,1)} %bitcast.3, s32[8,96]{1,0:T(8,128)} %bitcast.6, s32[8,768]{1,0:T(8,128)} %bitcast.5, s32[16]{0:T(128)} %slot_ref.1, f32[2,64,128]{2,1,0:T(8,128)} %meas_ref.1, ...), custom_call_target="tpu_custom_call" | custom-call | tf_op jit(solution)/shard_map/pallas_call | solution.py:333
  21.1 6.8 %shard_map.74 = f32[96,64,128]{2,1,0:T(8,128)} custom-call(bf16[256,128]{1,0:T(8,128)(2,1)} %get-tuple-element.8.resid_ref, bf16[4096,128]{1,0:T(8,128)(2,1)} %bitcast.4, bf16[768,1024]{1,0:T(8,128)(2,1)} %get-tuple-element.9.back_ref, f32[96,64,128]{2,1,0:T(8,128)} %get-tuple-element.10.base_ref), custom_call_target="tpu_custom_call" | custom-call | tf_op jit(solution)/shard_map/pallas_call | solution.py:374

commit v3 on v2

--- a/solution.py
+++ b/solution.py
@@ -41,7 +41,7 @@
     touch, owners, slabs, early,
     vol_ref, table_hbm, index_ref, block_ref, slot_ref, meas_ref, wt_ref,
     base_out, back_out, resid_ref,
-    table_ref, vv, vb, fwd, bwd, base, edge_lo, edge_hi, next_z, prev_z, prev_flux, upper,
+    table_ref, vv, vb, turned, fwd, bwd, base, edge_lo, edge_hi, next_z, prev_z, prev_flux, upper,
     send, recv, back_send, back_recv,
     load_sem, out_sem, halo_send, halo_recv, part_send, part_recv, res_send, res_recv,
 ):
@@ -64,11 +64,14 @@
     for peer in peers:
         pl.semaphore_signal(barrier, inc=1, device_id=peer, device_id_type=MESH)
 
-    parts = 4
-    piece = rows // parts
+    tiles = WIDE // px
+    parts = zt // tiles
+    some = tiles * SUB
     loads = [
         pltpu.make_async_copy(
-            vol_ref.at[pl.ds(c * piece, piece)], vv.at[pl.ds(1 + c * piece, piece)], load_sem.at[c]
+            vol_ref.at[:, pl.ds(c * some, some)],
+            vv.at[pl.ds(1, rows), pl.ds(c * some, some)],
+            load_sem.at[c],
         )
         for c in range(parts)
     ]
@@ -129,39 +132,36 @@
 
     for c in range(parts):
         loads[c].wait()
-        for z in range(zt):
-            part = vv[1 + c * piece : 1 + (c + 1) * piece, z * SUB : (z + 1) * SUB, :]
-            vb[c * piece * SUB : (c + 1) * piece * SUB, z * px : (z + 1) * px] = part.reshape(
-                piece * SUB, px
-            ).astype(BF16)
-    edge_lo[...] = vv[1 : rows + 1, 0, :]
-    edge_hi[...] = vv[1 : rows + 1, slices - 1, :]
-    more = [
-        halo(2, edge_lo, next_z.at[pl.ds(0, rows)], (z_prev, pos)),
-        halo(3, edge_hi, prev_z.at[pl.ds(0, rows)], (z_next, pos)),
-        halo(4, edge_hi.at[pl.ds(0, SUB)], prev_z.at[pl.ds(rows, SUB)], (z_next, t_prev)),
-        halo(5, edge_lo.at[pl.ds(rows - SUB, SUB)], next_z.at[pl.ds(rows, SUB)], (z_prev, t_next)),
-    ]
-    for copy in more:
-        copy.start()
-    halos += more
-
+        for z in range(c * tiles, (c + 1) * tiles):
+            part = vv[1 : rows + 1, z * SUB : (z + 1) * SUB, :]
+            vb[:, z * px : (z + 1) * px] = part.reshape(rows * SUB, px).astype(BF16)
+        more = []
+        if c == 0:
+            edge_lo[...] = vv[1 : rows + 1, 0, :]
+            more += [
+                halo(2, edge_lo, next_z.at[pl.ds(0, rows)], (z_prev, pos)),
+                halo(4, edge_lo.at[pl.ds(rows - SUB, SUB)], next_z.at[pl.ds(rows, SUB)], (z_prev, t_next)),
+            ]
+        if c == parts - 1:
+            edge_hi[...] = vv[1 : rows + 1, slices - 1, :]
+            more += [
+                halo(3, edge_hi, prev_z.at[pl.ds(0, rows)], (z_next, pos)),
+                halo(5, edge_hi.at[pl.ds(0, SUB)], prev_z.at[pl.ds(rows, SUB)], (z_next, t_prev)),
+            ]
+        for copy in more:
+            copy.start()
+        halos += more
+        summed = dot(fwd[...], vb[:, c * WIDE : (c + 1) * WIDE]).astype(BF16)
+        for f in range(nfoot):
+            for j in range(tiles):
+                at = (c * tiles + j) * ts
+                turned[at : at + ts, f * px : (f + 1) * px] = summed[
+                    f * ts : (f + 1) * ts, j * px : (j + 1) * px
+                ]
+    slab_halos = [halos[2], halos[4]]
+    tile_halos = [halos[0], halos[1], halos[3], halos[5]]
     load_table.wait()
-
-    per = WIDE // ts
-    total = jnp.zeros((zt * ts, rays), F32)
-    for c in range(nfoot // per):
-        summed = dot(fwd[c * WIDE : (c + 1) * WIDE, :], vb[...])
-        turned = jnp.concatenate(
-            [
-                jnp.concatenate(
-                    [summed[f * ts : (f + 1) * ts, z * px : (z + 1) * px] for z in range(zt)], axis=0
-                )
-                for f in range(per)
-            ],
-            axis=1,
-        ).astype(BF16)
-        total = total + dot(turned, table_ref[c * per * px : (c + 1) * per * px, :])
+    total = dot(turned[...], table_ref[...])
     total = total.reshape(zt, touch, SUB, rays)
     partial = [total[:, t].reshape(slices, rays) for t in range(touch)]
     for o in range(owners):
@@ -223,7 +223,7 @@
     def tv_step(i, flux):
         return tv_rows(i * TOGETHER, flux)
 
-    for copy in halos[2:4]:
+    for copy in slab_halos:
         copy.wait_recv()
     upper[...] = jnp.where(last_slice, edge_hi[...], next_z[0:rows, :])
     slice_flux(None)
@@ -252,7 +252,7 @@
         copy.start()
     back_recv[pl.ds(pos, 1)] = back_send[pl.ds(pos, 1)]
 
-    for copy in halos[:2] + halos[4:]:
+    for copy in tile_halos:
         copy.wait_recv()
     slice_flux(prev_z[rows : rows + 1, :])
     before = vv[0]
@@ -289,14 +289,17 @@
         copy.wait_send()
 
 
-def update_kernel(touch, resid_ref, table_ref, back_ref, base_ref, out_ref, grads):
-    rows, slices, px = base_ref.shape
+def update_kernel(touch, resid_ref, table_ref, back_hbm, base_ref, out_ref, back_ref, grads, sem):
+    rows, some, px = base_ref.shape
     nfoot = table_ref.shape[0] // px
-    zt = slices // SUB
+    steps = grads.shape[0]
+    tiles = some // SUB
     ts = touch * SUB
+    load = pltpu.make_async_copy(back_hbm, back_ref, sem)
 
     @pl.when(pl.program_id(0) == 0)
     def _():
+        load.start()
         per = WIDE // px
         for c in range(nfoot // per):
             piece = lax.dot_general(
@@ -304,16 +307,18 @@
                 table_ref[c * WIDE : (c + 1) * WIDE, :],
                 (((1,), (1,)), ((), ())),
                 preferred_element_type=F32,
-            )
+            ).astype(BF16)
             for f in range(per):
-                for z in range(zt):
-                    at = (c * per + f) * ts
-                    grads[at : at + ts, z * px : (z + 1) * px] = piece[
+                at = (c * per + f) * ts
+                for z in range(steps * tiles):
+                    j = z % tiles
+                    grads[z // tiles, at : at + ts, j * px : (j + 1) * px] = piece[
                         z * ts : (z + 1) * ts, f * px : (f + 1) * px
-                    ].astype(BF16)
-
-    grad = dot(back_ref[...], grads[...])
-    for z in range(zt):
+                    ]
+        load.wait()
+
+    grad = dot(back_ref[...], grads[pl.program_id(0)])
+    for z in range(tiles):
         at = slice(z * SUB, (z + 1) * SUB)
         one = grad[:, z * px : (z + 1) * px].reshape(rows, SUB, px)
         out_ref[:, at, :] = jnp.maximum(base_ref[:, at, :] - step_length * one, 0.0)
@@ -343,6 +348,7 @@
             pltpu.VMEM(table.shape, BF16),
             pltpu.VMEM((rows + 2, slices, px), F32),
             pltpu.VMEM((rows * SUB, zt * px), BF16),
+            pltpu.VMEM((zt * touch * SUB, nfoot * px), BF16),
             pltpu.VMEM((keys * SUB, rows * SUB), BF16),
             pltpu.VMEM((rows * SUB, keys * SUB), BF16),
             pltpu.VMEM((rows, slices, px), F32),
@@ -356,7 +362,7 @@
             pltpu.VMEM((owners, slices, rays), WIRE),
             pltpu.VMEM((owners, slices, rays), BF16),
             pltpu.VMEM((owners, slices, rays), BF16),
-            dma((5,)),
+            dma((zt * px // WIDE + 1,)),
             dma((2,)),
             dma((6,)),
             dma((6,)),
@@ -369,8 +375,8 @@
             collective_id=0, has_side_effects=True, vmem_limit_bytes=VMEM_LIMIT
         ),
     )(volume, table, foot_index.T, ray_block.T, ray_slot, measured, weights)
-    steps = 4
-    some = rows // steps
+    some = WIDE // px * SUB
+    steps = slices // some
     return pl.pallas_call(
         functools.partial(update_kernel, touch),
         grid=(steps,),
@@ -378,11 +384,15 @@
         in_specs=[
             pl.BlockSpec(resid.shape, lambda i: (0, 0)),
             pl.BlockSpec(table.shape, lambda i: (0, 0)),
-            pl.BlockSpec((some * SUB, keys * SUB), lambda i: (i, 0)),
-            pl.BlockSpec((some, slices, px), lambda i: (i, 0, 0)),
+            any_space,
+            pl.BlockSpec((rows, some, px), lambda i: (0, i, 0)),
         ],
-        out_specs=pl.BlockSpec((some, slices, px), lambda i: (i, 0, 0)),
-        scratch_shapes=[pltpu.VMEM((keys * SUB, zt * px), BF16)],
+        out_specs=pl.BlockSpec((rows, some, px), lambda i: (0, i, 0)),
+        scratch_shapes=[
+            pltpu.VMEM(back.shape, BF16),
+            pltpu.VMEM((steps, keys * SUB, WIDE), BF16),
+            dma(()),
+        ],
         compiler_params=pltpu.CompilerParams(vmem_limit_bytes=VMEM_LIMIT),
     )(resid, table, back, base)
 

time: 28.1 us -> 30.6 us (1.089)
  Pallas kernels: 27.9 us -> 30.3 us
    pallas_call x1, Pallas kernels: 21.1 us -> 23.2 us  [per_device(): pl.pallas_call(functools.partial(exchange_kernel, touch, owners, slabs, r...]
    pallas_call x1, Pallas kernels: 6.81 us -> 7.12 us  [per_device(): pl.pallas_call(functools.partial(update_kernel, touch), grid=(steps,), ou...]
where the time goes in v3:
time: 30.6 us; the launch traced here: 30.3 us
  Pallas kernels  30.3 us (99%)
    pallas_call x1, Pallas kernels, per_device(): pl.pallas_call(functools.partial(exchange_kernel, touch, owners, slabs, r...  23.2 us
    pallas_call x1, Pallas kernels, per_device(): pl.pallas_call(functools.partial(update_kernel, touch), grid=(steps,), ou...  7.12 us

profile of v3, /device:TPU:0, one launch (start us, length us, event | category | flops | bytes accessed | tf_op | source)
XLA Modules:
  0.0 30.3 jit_solution(15830338491275050064)
XLA Ops:
  0.0 23.2 %shard_map.73 = (f32[96,64,128]{2,1,0:T(8,128)}, bf16[768,1024]{1,0:T(8,128)(2,1)}, bf16[256,128]{1,0:T(8,128)(2,1)}) custom-call(f32[96,64,128]{2,1,0:T(8,128)} %vol_ref.1, bf16[4096,128]{1,0:T(8,128)(2,1)} %bitcast.3, s32[8,96]{1,0:T(8,128)} %bitcast.6, s32[8,768]{1,0:T(8,128)} %bitcast.5, s32[16]{0:T(128)} %slot_ref.1, f32[2,64,128]{2,1,0:T(8,128)} %meas_ref.1, ...), custom_call_target="tpu_custom_call" | custom-call | tf_op jit(solution)/shard_map/pallas_call | solution.py:338
  23.2 7.1 %shard_map.74 = f32[96,64,128]{2,1,0:T(8,128)} custom-call(bf16[256,128]{1,0:T(8,128)(2,1)} %get-tuple-element.8.resid_ref, bf16[4096,128]{1,0:T(8,128)(2,1)} %bitcast.4, bf16[768,1024]{1,0:T(8,128)(2,1)} %get-tuple-element.9.back_hbm, f32[96,64,128]{2,1,0:T(8,128)} %get-tuple-element.10.base_ref), custom_call_target="tpu_custom_call" | custom-call | tf_op jit(solution)/shard_map/pallas_call | solution.py:380

commit v4 on v2

--- a/solution.py
+++ b/solution.py
@@ -369,8 +369,8 @@
             collective_id=0, has_side_effects=True, vmem_limit_bytes=VMEM_LIMIT
         ),
     )(volume, table, foot_index.T, ray_block.T, ray_slot, measured, weights)
-    steps = 4
-    some = rows // steps
+    some = math.gcd(rows, WIDE // SUB)
+    steps = rows // some
     return pl.pallas_call(
         functools.partial(update_kernel, touch),
         grid=(steps,),

time: 28.1 us -> 28.3 us (level)
  no operation moved by 1% of the time
where the time goes in v4:
time: 28.3 us; the launch traced here: 28.1 us
  Pallas kernels  28.1 us (99%)
    pallas_call x1, Pallas kernels, per_device(): pl.pallas_call(functools.partial(exchange_kernel, touch, owners, slabs, r...  21.1 us
    pallas_call x1, Pallas kernels, per_device(): pl.pallas_call(functools.partial(update_kernel, touch), grid=(steps,), ou...  7.02 us

profile of v4, /device:TPU:0, one launch (start us, length us, event | category | flops | bytes accessed | tf_op | source)
XLA Modules:
  0.0 28.1 jit_solution(9878327027281225542)
XLA Ops:
  0.0 21.1 %shard_map.73 = (f32[96,64,128]{2,1,0:T(8,128)}, bf16[768,1024]{1,0:T(8,128)(2,1)}, bf16[256,128]{1,0:T(8,128)(2,1)}) custom-call(f32[96,64,128]{2,1,0:T(8,128)} %vol_ref.1, bf16[4096,128]{1,0:T(8,128)(2,1)} %bitcast.3, s32[8,96]{1,0:T(8,128)} %bitcast.6, s32[8,768]{1,0:T(8,128)} %bitcast.5, s32[16]{0:T(128)} %slot_ref.1, f32[2,64,128]{2,1,0:T(8,128)} %meas_ref.1, ...), custom_call_target="tpu_custom_call" | custom-call | tf_op jit(solution)/shard_map/pallas_call | solution.py:333
  21.1 7.0 %shard_map.74 = f32[96,64,128]{2,1,0:T(8,128)} custom-call(bf16[256,128]{1,0:T(8,128)(2,1)} %get-tuple-element.8.resid_ref, bf16[4096,128]{1,0:T(8,128)(2,1)} %bitcast.4, bf16[768,1024]{1,0:T(8,128)(2,1)} %get-tuple-element.9.back_ref, f32[96,64,128]{2,1,0:T(8,128)} %get-tuple-element.10.base_ref), custom_call_target="tpu_custom_call" | custom-call | tf_op jit(solution)/shard_map/pallas_call | solution.py:374
